TPU v7x, 128 devices: a whole 4x4x4 slice. The times are simulated.
128 devices in a mesh: row: 8 (over z, core), col: 16 (over y, x).
Axes of the slice: x: 4, y: 4, z: 4, core: 2. Of those that a mesh axis runs over, the one named last changes fastest.
Arguments:
- image: float32 [32, 32, 64, 128], P('row', 'col'), may hold values from -6 to 6
- u_factors: bfloat16 [40, 64, 1024, 256], P('row', 'col'), may hold values from -0.0625 to 0.0625
- v_factors: bfloat16 [40, 64, 1024, 256], P('row', 'col'), may hold values from -0.1875 to 0.1875
- ranks: int32 [40, 64], P('row', 'col'), may hold values from 16 to 256
- measured: bfloat16 [40960, 128], P('row'), may hold values from -6 to 6
Outputs:
- new_image: float32 [32, 32, 64, 128], P('row', 'col')
All inputs are finite; a program needn't handle non-finite values.
Results may differ from a plain program's by a relative error of at most 0.0051.
Values may be sent and summed in bfloat16 or wider, within the bound.
A program may use at most 128 MiB of HBM per device.

v0:
```python
import jax
import jax.numpy as jnp
from jax import lax
from jax.sharding import PartitionSpec as P

diff_rate = 0.12
edge_scale = 0.5


def padded_2(block, sides, width):
    for axis, dim in sides:
        count = lax.axis_size(axis)
        forward = [(i, i + 1) for i in range(count - 1)]
        backward = [(target, source) for source, target in forward]
        low = lax.ppermute(
            lax.slice_in_dim(block, block.shape[dim] - width, None, axis=dim), axis, forward
        )
        high = lax.ppermute(lax.slice_in_dim(block, 0, width, axis=dim), axis, backward)
        block = jnp.concatenate([low, block, high], axis=dim)
    return block


def flux(delta):
    scaled = delta / edge_scale
    return delta / (1.0 + scaled * scaled)


def diffuse_margin(extended):
    padded = jnp.pad(extended, ((0, 0), (0, 0), (1, 1), (0, 0)))
    center = padded[1:-1, 1:-1, 1:-1]
    total = flux(padded[2:, 1:-1, 1:-1] - center) + flux(padded[:-2, 1:-1, 1:-1] - center)
    total = total + flux(padded[1:-1, 2:, 1:-1] - center) + flux(padded[1:-1, :-2, 1:-1] - center)
    total = total + flux(padded[1:-1, 1:-1, 2:] - center) + flux(padded[1:-1, 1:-1, :-2] - center)
    return center + diff_rate * total


def body(image, u_factors, v_factors, ranks, measured):
    row_tiles, col_tiles, tile_len, rank_max = u_factors.shape
    frames = image.shape[3]
    whole = lax.all_gather(image.astype(jnp.bfloat16), "row", axis=0, tiled=True)
    xtiles = whole.reshape(col_tiles, tile_len, frames)
    levels = lax.broadcasted_iota(jnp.int32, (row_tiles, col_tiles, rank_max), 2)
    mask = (levels < ranks[:, :, None]).astype(jnp.float32)
    coef = jnp.einsum("ijkr,jkf->ijrf", v_factors, xtiles, preferred_element_type=jnp.float32)
    coef = (coef * mask[:, :, :, None]).astype(jnp.bfloat16)
    partial_value = jnp.einsum(
        "ijkr,ijrf->ikf", u_factors, coef, preferred_element_type=jnp.float32
    )
    partial_value = partial_value.reshape(row_tiles * tile_len, frames)
    total = lax.psum(partial_value, "col")
    resid = (total - measured.astype(jnp.float32)).astype(jnp.bfloat16)
    resid = resid.reshape(row_tiles, tile_len, frames)
    back = jnp.einsum("ijkr,ikf->ijrf", u_factors, resid, preferred_element_type=jnp.float32)
    back = (back * mask[:, :, :, None]).astype(jnp.bfloat16)
    grad_terms = jnp.einsum("ijkr,ijrf->jkf", v_factors, back, preferred_element_type=jnp.float32)
    grad_terms = grad_terms.reshape(col_tiles * tile_len, frames)
    gradient = lax.psum_scatter(grad_terms, "row", scatter_dimension=0, tiled=True)
    moved = image - gradient.reshape(image.shape)
    for step in range(2):
        extended = padded_2(moved, (("row", 0), ("col", 1)), 1)
        moved = diffuse_margin(extended)
    return moved


def solution(mesh):
    placed = (
        P("row", "col", None, None),
        P("row", "col", None, None),
        P("row", "col", None, None),
        P("row", "col"),
        P("row", None),
    )
    return jax.shard_map(
        body, mesh=mesh, in_specs=placed, out_specs=P("row", "col", None, None), check_vma=False
    )
```

profile of v0, /device:TPU:25, one launch (start us, length us, event | category | flops | bytes accessed | tf_op | source)
XLA Modules:
  0.0 237.7 jit_solution(13111002786819206620)
XLA Ops:
  6.5 0.0 all-gather.2.cloned.1.call-start
  6.5 1.6 convert_element_type.28
  8.2 0.0 all-gather.2.cloned.1.call-update
  8.2 0.0 all-reduce.4.cloned.1.call-start
  8.2 0.8 copy.20
  9.0 0.1 fusion.25
  9.1 26.1 %all-gather.2.cloned.1.call-done = bf16[32,2,64,128]{3,2,1,0:T(8,128)(2,1)} async-done(((bf16[4,2,64,128]{3,2,1,0:T(8,128)(2,1)}), bf16[32,2,64,128]{3,2,1,0:T(8,128)(2,1)}) %all-gather.2.cloned.1.call-update) | async-done | bytes 1048592 | tf_op jit(solution)/shard_map/all_gather | solution.py:40
  35.2 11.8 %convolution_bitcast_fusion = f32[5,1024,128]{1,2,0:T(8,128)S(1)} fusion(bf16[5,4,1024,256]{3,2,1,0:T(8,128)(2,1)} %param.6, bf16[4,1024,128,1]{2,1,0,3:T(8,128)(2,1)} %bitcast.33, bf16[5,4,1024,256]{3,2,1,0:T(8,128)(2,1)} %param.7, f32[5,4,256]{2,1,0:T(4,128)S(1)} %fusion.25), kind=kOutput, calls=%fused_computation.8 | convolution fusion | flops 2685665280 | bytes 24662016 | tf_op jit(solution)/shard_map/ijkr,ijrf->ikf/dot_general | solution.py:46
  47.0 2.1 copy.21
  49.1 0.0 copy-start
  49.1 0.0 all-reduce.4.cloned.1.call-update
  49.2 0.0 reduce-scatter.2.cloned.1.call-start
  49.2 90.6 %all-reduce.4.cloned.1.call-done = f32[5120,128]{1,0:T(8,128)} async-done(((f32[5120,128]{1,0:T(8,128)}), f32[5120,128]{1,0:T(8,128)}) %all-reduce.4.cloned.1.call-update) | async-done | bytes 2621456 | tf_op jit(solution)/shard_map/psum | solution.py:50
  139.8 0.0 copy-done
  139.8 2.0 subtract_convert_fusion
  141.8 9.7 %fusion.7 = f32[4,1024,128]{1,2,0:T(8,128)S(1)} fusion(bf16[5,4,1024,256]{3,2,1,0:T(8,128)(2,1)} %param.7, bf16[5,1024,128,1]{2,1,0,3:T(8,128)(2,1)S(1)} %bitcast.36, bf16[5,4,1024,256]{3,2,1,0:T(8,128)(2,1)} %param.6, f32[5,4,256]{2,0,1:T(8,128)S(1)} %copy.24), kind=kOutput, calls=%fused_computation.9 | convolution fusion | flops 2685665280 | bytes 24399872 | tf_op jit(solution)/shard_map/ijkr,ijrf->jkf/dot_general | solution.py:55
  151.5 0.0 copy-start.1
  151.5 1.8 copy.26
  153.4 0.0 reduce-scatter.2.cloned.1.call-update
  153.4 31.9 %reduce-scatter.2.cloned.1.call-done = f32[512,128]{1,0:T(8,128)} async-done(((f32[4096,128]{1,0:T(8,128)}), f32[512,128]{1,0:T(8,128)}) %reduce-scatter.2.cloned.1.call-update) | async-done | bytes 262160 | tf_op jit(solution)/shard_map/reduce_scatter | solution.py:57
  185.3 0.0 copy-done.1
  185.3 1.0 sub.43
  186.3 5.6 %collective-permute-start = (f32[1,2,64,128]{3,2,1,0:T(8,128)S(1)}, f32[1,2,64,128]{3,2,1,0:T(8,128)S(1)}, u32[]{:S(2)}, u32[]{:S(2)}) collective-permute-start(f32[1,2,64,128]{3,2,1,0:T(8,128)S(1)} %get-tuple-element.12), channel_id=1, source_target_pairs={{16,0},{32,16},{48,32},{64,48},{80,64},{96,80},{112,96},{17,1},{33... | collective-permute-start | bytes 196616 | tf_op jit(solution)/shard_map/ppermute | solution.py:18
  192.0 1.9 collective-permute-start.1
  193.9 0.0 collective-permute-done
  193.9 1.3 collective-permute-done.1
  195.3 4.5 %collective-permute-start.2 = (f32[6,1,64,128]{3,2,1,0:T(8,128)S(1)}, f32[6,1,64,128]{3,2,1,0:T(8,128)S(1)}, u32[]{:S(2)}, u32[]{:S(2)}) collective-permute-start(f32[6,1,64,128]{3,2,1,0:T(8,128)S(1)} %get-tuple-element.8), channel_id=1, source_target_pairs={{1,0},{2,1},{3,2},{4,3},{5,4},{6,5},{7,6},{8,7},{9,8},{10,9},{11,1... | collective-permute-start | bytes 589832 | tf_op jit(solution)/shard_map/ppermute | solution.py:18
  199.8 1.9 collective-permute-start.3
  201.7 2.3 collective-permute-done.2
  204.0 5.9 %collective-permute-done.3 = f32[6,1,64,128]{3,2,1,0:T(8,128)S(1)} collective-permute-done((f32[6,1,64,128]{3,2,1,0:T(8,128)S(1)}, f32[6,1,64,128]{3,2,1,0:T(8,128)S(1)}, u32[]{:S(2)}, u32[]{:S(2)}) %collective-permute-start.3) | collective-permute-done | bytes 196640 | tf_op jit(solution)/shard_map/ppermute | solution.py:15
  209.9 0.1 select_maximum_fusion.4
  210.0 0.4 multiply_add_fusion.1
  210.5 3.1 %collective-permute-start.4 = (f32[1,2,64,128]{3,2,1,0:T(8,128)S(1)}, f32[1,2,64,128]{3,2,1,0:T(8,128)S(1)}, u32[]{:S(2)}, u32[]{:S(2)}) collective-permute-start(f32[1,2,64,128]{3,2,1,0:T(8,128)S(1)} %get-tuple-element.10), channel_id=1, source_target_pairs={{16,0},{32,16},{48,32},{64,48},{80,64},{96,80},{112,96},{17,1},{33... | collective-permute-start | bytes 196616 | tf_op jit(solution)/shard_map/ppermute | solution.py:18
  213.6 2.9 %collective-permute-start.5 = (f32[1,2,64,128]{3,2,1,0:T(8,128)S(1)}, f32[1,2,64,128]{3,2,1,0:T(8,128)S(1)}, u32[]{:S(2)}, u32[]{:S(2)}) collective-permute-start(f32[1,2,64,128]{3,2,1,0:T(8,128)S(1)} %get-tuple-element.9), channel_id=1, source_target_pairs={{0,16},{16,32},{32,48},{48,64},{64,80},{80,96},{96,112},{1,17},{17... | collective-permute-start | bytes 196616 | tf_op jit(solution)/shard_map/ppermute | solution.py:15
  216.5 0.0 collective-permute-done.4
  216.5 1.3 collective-permute-done.5
  217.9 1.9 collective-permute-start.6
  219.8 3.4 %collective-permute-start.7 = (f32[6,1,64,128]{3,2,1,0:T(8,128)S(1)}, f32[6,1,64,128]{3,2,1,0:T(8,128)S(1)}, u32[]{:S(2)}, u32[]{:S(2)}) collective-permute-start(f32[6,1,64,128]{3,2,1,0:T(8,128)S(1)} %get-tuple-element.5), channel_id=1, source_target_pairs={{0,1},{1,2},{2,3},{3,4},{4,5},{5,6},{6,7},{7,8},{8,9},{9,10},{10,1... | collective-permute-start | bytes 589832 | tf_op jit(solution)/shard_map/ppermute | solution.py:15
  223.2 3.1 %collective-permute-done.6 = f32[6,1,64,128]{3,2,1,0:T(8,128)S(1)} collective-permute-done((f32[6,1,64,128]{3,2,1,0:T(8,128)S(1)}, f32[6,1,64,128]{3,2,1,0:T(8,128)S(1)}, u32[]{:S(2)}, u32[]{:S(2)}) %collective-permute-start.6) | collective-permute-done | bytes 196640 | tf_op jit(solution)/shard_map/ppermute | solution.py:18
  226.2 3.7 %collective-permute-done.7 = f32[6,1,64,128]{3,2,1,0:T(8,128)S(1)} collective-permute-done((f32[6,1,64,128]{3,2,1,0:T(8,128)S(1)}, f32[6,1,64,128]{3,2,1,0:T(8,128)S(1)}, u32[]{:S(2)}, u32[]{:S(2)}) %collective-permute-start.7) | collective-permute-done | bytes 196640 | tf_op jit(solution)/shard_map/ppermute | solution.py:15
  230.0 0.1 select_maximum_fusion
  230.1 1.1 multiply_add_fusion
  (7 shorter events, 0.1 us)
Async XLA Ops:
  6.5 28.7 %all-gather.2.cloned.1.call-start = ((), (), s32[]{:S(2)}) async-start(), calls=%async_computation.1 | async-start | bytes 1179648 | tf_op jit(solution)/shard_map/all_gather | solution.py:40
  8.2 131.6 %all-reduce.4.cloned.1.call-start = ((), (), s32[]{:S(2)}) async-start(), calls=%async_computation.2 | async-start | bytes 5242880 | tf_op jit(solution)/shard_map/psum | solution.py:50
  49.1 90.7 %copy-start = (bf16[5120,128]{1,0:T(8,128)(2,1)S(1)}, bf16[5120,128]{1,0:T(8,128)(2,1)}, u32[]{:S(2)}) copy-start(bf16[5120,128]{1,0:T(8,128)(2,1)} %param.9) | copy-start | bytes 3932164
  49.2 136.2 %reduce-scatter.2.cloned.1.call-start = ((), (), s32[]{:S(2)}) async-start(), calls=%async_computation.3 | async-start | bytes 2359296 | tf_op jit(solution)/shard_map/reduce_scatter | solution.py:57
  151.5 33.8 %copy-start.1 = (f32[4,2,64,128]{3,2,1,0:T(8,128)S(1)}, f32[4,2,64,128]{3,2,1,0:T(8,128)}, u32[]{:S(2)}) copy-start(f32[4,2,64,128]{3,2,1,0:T(8,128)} %param.5) | copy-start | bytes 786436
  186.3 7.6 %collective-permute-start = (f32[1,2,64,128]{3,2,1,0:T(8,128)S(1)}, f32[1,2,64,128]{3,2,1,0:T(8,128)S(1)}, u32[]{:S(2)}, u32[]{:S(2)}) collective-permute-start(f32[1,2,64,128]{3,2,1,0:T(8,128)S(1)} %get-tuple-element.12), channel_id=1, source_target_pairs={{16,0},{32,16},{48,32},{64,48},{80,64},{96,80},{112,96},{17,1},{33... | collective-permute-start | bytes 196616 | tf_op jit(solution)/shard_map/ppermute | solution.py:18
  192.0 3.2 %collective-permute-start.1 = (f32[1,2,64,128]{3,2,1,0:T(8,128)S(1)}, f32[1,2,64,128]{3,2,1,0:T(8,128)S(1)}, u32[]{:S(2)}, u32[]{:S(2)}) collective-permute-start(f32[1,2,64,128]{3,2,1,0:T(8,128)S(1)} %get-tuple-element.11), channel_id=1, source_target_pairs={{0,16},{16,32},{32,48},{48,64},{64,80},{80,96},{96,112},{1,17},{17... | collective-permute-start | bytes 196616 | tf_op jit(solution)/shard_map/ppermute | solution.py:15
  195.3 8.8 %collective-permute-start.2 = (f32[6,1,64,128]{3,2,1,0:T(8,128)S(1)}, f32[6,1,64,128]{3,2,1,0:T(8,128)S(1)}, u32[]{:S(2)}, u32[]{:S(2)}) collective-permute-start(f32[6,1,64,128]{3,2,1,0:T(8,128)S(1)} %get-tuple-element.8), channel_id=1, source_target_pairs={{1,0},{2,1},{3,2},{4,3},{5,4},{6,5},{7,6},{8,7},{9,8},{10,9},{11,1... | collective-permute-start | bytes 589832 | tf_op jit(solution)/shard_map/ppermute | solution.py:18
  199.8 10.1 %collective-permute-start.3 = (f32[6,1,64,128]{3,2,1,0:T(8,128)S(1)}, f32[6,1,64,128]{3,2,1,0:T(8,128)S(1)}, u32[]{:S(2)}, u32[]{:S(2)}) collective-permute-start(f32[6,1,64,128]{3,2,1,0:T(8,128)S(1)} %get-tuple-element.7), channel_id=1, source_target_pairs={{0,1},{1,2},{2,3},{3,4},{4,5},{5,6},{6,7},{7,8},{8,9},{9,10},{10,1... | collective-permute-start | bytes 589832 | tf_op jit(solution)/shard_map/ppermute | solution.py:15
  210.5 6.0 %collective-permute-start.4 = (f32[1,2,64,128]{3,2,1,0:T(8,128)S(1)}, f32[1,2,64,128]{3,2,1,0:T(8,128)S(1)}, u32[]{:S(2)}, u32[]{:S(2)}) collective-permute-start(f32[1,2,64,128]{3,2,1,0:T(8,128)S(1)} %get-tuple-element.10), channel_id=1, source_target_pairs={{16,0},{32,16},{48,32},{64,48},{80,64},{96,80},{112,96},{17,1},{33... | collective-permute-start | bytes 196616 | tf_op jit(solution)/shard_map/ppermute | solution.py:18
  213.6 4.2 %collective-permute-start.5 = (f32[1,2,64,128]{3,2,1,0:T(8,128)S(1)}, f32[1,2,64,128]{3,2,1,0:T(8,128)S(1)}, u32[]{:S(2)}, u32[]{:S(2)}) collective-permute-start(f32[1,2,64,128]{3,2,1,0:T(8,128)S(1)} %get-tuple-element.9), channel_id=1, source_target_pairs={{0,16},{16,32},{32,48},{48,64},{64,80},{80,96},{96,112},{1,17},{17... | collective-permute-start | bytes 196616 | tf_op jit(solution)/shard_map/ppermute | solution.py:15
  217.9 8.4 %collective-permute-start.6 = (f32[6,1,64,128]{3,2,1,0:T(8,128)S(1)}, f32[6,1,64,128]{3,2,1,0:T(8,128)S(1)}, u32[]{:S(2)}, u32[]{:S(2)}) collective-permute-start(f32[6,1,64,128]{3,2,1,0:T(8,128)S(1)} %get-tuple-element.6), channel_id=1, source_target_pairs={{1,0},{2,1},{3,2},{4,3},{5,4},{6,5},{7,6},{8,7},{9,8},{10,9},{11,1... | collective-permute-start | bytes 589832 | tf_op jit(solution)/shard_map/ppermute | solution.py:18
  219.8 10.2 %collective-permute-start.7 = (f32[6,1,64,128]{3,2,1,0:T(8,128)S(1)}, f32[6,1,64,128]{3,2,1,0:T(8,128)S(1)}, u32[]{:S(2)}, u32[]{:S(2)}) collective-permute-start(f32[6,1,64,128]{3,2,1,0:T(8,128)S(1)} %get-tuple-element.5), channel_id=1, source_target_pairs={{0,1},{1,2},{2,3},{3,4},{4,5},{5,6},{6,7},{7,8},{8,9},{9,10},{10,1... | collective-permute-start | bytes 589832 | tf_op jit(solution)/shard_map/ppermute | solution.py:15
Sparse Core Ops, SparseCore 0:
  9.1 26.1 all-gather.1
  49.3 90.4 all-reduce.3
  153.5 31.7 reduce-scatter.1
where the time goes:
time: 238 us
  waiting for transfers between devices  166 us (70%)
  starting transfers between devices  25.4 us (11%)
  matrix products  21.5 us (9%)
  between operations  13.3 us (6%)
  other arithmetic  6.4 us (3%)
  local copies, waits for them, and re-layouts  4.83 us (2%)
    psum x1, waiting for transfers between devices, body(): total = lax.psum(partial_value, 'col')  90.6 us
    reduce_scatter x1, waiting for transfers between devices, body(): lax.psum_scatter(grad_terms, 'row', scatter_dimension=0, tiled=True)  31.9 us
    all_gather x1, waiting for transfers between devices, body(): lax.all_gather(image.astype(jnp.bfloat16), 'row', axis=0, tiled=True)  26.1 us
    ppermute x4, starting transfers between devices, padded_2(): lax.ppermute(lax.slice_in_dim(block, 0, width, axis=dim), axis, backward)  15.2 us
    ppermute x4, waiting for transfers between devices, padded_2(): lax.ppermute(lax.slice_in_dim(block, block.shape[dim] - width, None, axis...  12.2 us
    dot_general x1, matrix products, body(): jnp.einsum('ijkr,ijrf->ikf', u_factors, coef, preferred_element_type=jnp....  11.8 us
    ppermute x4, starting transfers between devices, padded_2(): lax.ppermute(lax.slice_in_dim(block, block.shape[dim] - width, None, axis...  10.1 us
    dot_general x1, matrix products, body(): jnp.einsum('ijkr,ijrf->jkf', v_factors, back, preferred_element_type=jnp....  9.72 us
  transfers between devices with their start and end apart: 11, of which 9 were waited for; matrix products, arithmetic and copies ran while one was open for 0% of the time, Pallas kernels for 0%

commit v1 on v0

--- a/solution.py
+++ b/solution.py
@@ -47,7 +47,7 @@
         "ijkr,ijrf->ikf", u_factors, coef, preferred_element_type=jnp.float32
     )
     partial_value = partial_value.reshape(row_tiles * tile_len, frames)
-    total = lax.psum(partial_value, "col")
+    total = jnp.sum(lax.all_gather(partial_value, "col"), axis=0)
     resid = (total - measured.astype(jnp.float32)).astype(jnp.bfloat16)
     resid = resid.reshape(row_tiles, tile_len, frames)
     back = jnp.einsum("ijkr,ikf->ijrf", u_factors, resid, preferred_element_type=jnp.float32)

time: 238 us -> 401 us (1.68)
  waiting for transfers between devices: 166 us -> 314 us
  other arithmetic: 6.4 us -> 21.5 us
    all_gather x0 -> x1, waiting for transfers between devices: none -> 239 us  [body(): total = jnp.sum(lax.all_gather(partial_value, 'col'), axis=0)]
    psum x1 -> x0, waiting for transfers between devices: 90.6 us -> none  [body(): total = lax.psum(partial_value, 'col')]
    reduce_sum x0 -> x1, other arithmetic: none -> 14.4 us  [body(): total = jnp.sum(lax.all_gather(partial_value, 'col'), axis=0)]
where the time goes in v1:
time: 401 us
  waiting for transfers between devices  314 us (78%)
  starting transfers between devices  25.5 us (6%)
  matrix products  21.8 us (5%)
  other arithmetic  21.5 us (5%)
  between operations  13.3 us (3%)
  local copies, waits for them, and re-layouts  4.81 us (1%)
    all_gather x1, waiting for transfers between devices, body(): total = jnp.sum(lax.all_gather(partial_value, 'col'), axis=0)  239 us
    reduce_scatter x1, waiting for transfers between devices, body(): lax.psum_scatter(grad_terms, 'row', scatter_dimension=0, tiled=True)  30.6 us
    all_gather x1, waiting for transfers between devices, body(): lax.all_gather(image.astype(jnp.bfloat16), 'row', axis=0, tiled=True)  26.1 us
    ppermute x4, starting transfers between devices, padded_2(): lax.ppermute(lax.slice_in_dim(block, 0, width, axis=dim), axis, backward)  15.3 us
    reduce_sum x1, other arithmetic, body(): total = jnp.sum(lax.all_gather(partial_value, 'col'), axis=0)  14.4 us
    ppermute x4, waiting for transfers between devices, padded_2(): lax.ppermute(lax.slice_in_dim(block, block.shape[dim] - width, None, axis...  12.2 us
    dot_general x1, matrix products, body(): jnp.einsum('ijkr,ijrf->ikf', u_factors, coef, preferred_element_type=jnp....  11.8 us
    ppermute x4, starting transfers between devices, padded_2(): lax.ppermute(lax.slice_in_dim(block, block.shape[dim] - width, None, axis...  10.1 us
  transfers between devices with their start and end apart: 11, of which 9 were waited for; matrix products, arithmetic and copies ran while one was open for 0% of the time, Pallas kernels for 0%

profile of v1, /device:TPU:25, one launch (start us, length us, event | category | flops | bytes accessed | tf_op | source)
XLA Modules:
  0.0 400.7 jit_solution(1190168940283452592)
XLA Ops:
  6.5 0.0 all-gather.3.cloned.1.call-start
  6.5 1.6 convert_element_type.28
  8.2 0.0 all-gather.3.cloned.1.call-update
  8.2 0.0 all-gather.5.cloned.1.call-start
  8.2 0.8 copy.20
  9.0 0.1 fusion.25
  9.1 26.1 %all-gather.3.cloned.1.call-done = bf16[32,2,64,128]{3,2,1,0:T(8,128)(2,1)} async-done(((bf16[4,2,64,128]{3,2,1,0:T(8,128)(2,1)}), bf16[32,2,64,128]{3,2,1,0:T(8,128)(2,1)}) %all-gather.3.cloned.1.call-update) | async-done | bytes 1048592 | tf_op jit(solution)/shard_map/all_gather | solution.py:40
  35.2 11.8 %convolution_bitcast_fusion = f32[5,1024,128]{1,2,0:T(8,128)S(1)} fusion(bf16[5,4,1024,256]{3,2,1,0:T(8,128)(2,1)} %param.6, bf16[4,1024,128,1]{2,1,0,3:T(8,128)(2,1)} %bitcast.33, bf16[5,4,1024,256]{3,2,1,0:T(8,128)(2,1)} %param.7, f32[5,4,256]{2,1,0:T(4,128)S(1)} %fusion.25), kind=kOutput, calls=%fused_computation.8 | convolution fusion | flops 2685665280 | bytes 24662016 | tf_op jit(solution)/shard_map/ijkr,ijrf->ikf/dot_general | solution.py:46
  47.0 2.1 copy.21
  49.1 0.0 all-gather.5.cloned.1.call-update
  49.1 0.0 reduce-scatter.2.cloned.1.call-start
  49.2 239.3 %all-gather.5.cloned.1.call-done = f32[16,5120,128]{2,1,0:T(8,128)} async-done(((f32[1,5120,128]{2,1,0:T(8,128)}), f32[16,5120,128]{2,1,0:T(8,128)}) %all-gather.5.cloned.1.call-update) | async-done | bytes 41943056 | tf_op jit(solution)/shard_map/all_gather | solution.py:50
  288.5 14.4 %reduce_sum.9 = f32[5120,128]{1,0:T(8,128)S(1)} reduce(f32[16,5120,128]{2,1,0:T(8,128)} %all-gather.5.cloned.1.call-done, f32[]{:T(128)} %constant.18.clone.1), dimensions={0}, to_apply=%region_0.0 | reduce | flops 9830400 | bytes 44564484 | tf_op jit(solution)/shard_map/reduce_sum | solution.py:50
  303.0 2.6 subtract_convert_fusion
  305.6 10.1 %fusion.7 = f32[4,1024,128]{1,2,0:T(8,128)S(1)} fusion(bf16[5,4,1024,256]{3,2,1,0:T(8,128)(2,1)} %param.7, bf16[5,1024,128,1]{2,1,0,3:T(8,128)(2,1)} %bitcast.36, bf16[5,4,1024,256]{3,2,1,0:T(8,128)(2,1)} %param.6, f32[5,4,256]{2,0,1:T(8,128)S(1)} %copy.24), kind=kOutput, calls=%fused_computation.9 | convolution fusion | flops 2685665280 | bytes 24399872 | tf_op jit(solution)/shard_map/ijkr,ijrf->jkf/dot_general | solution.py:55
  315.7 0.0 copy-start
  315.7 1.8 copy.26
  317.5 0.0 reduce-scatter.2.cloned.1.call-update
  317.5 30.6 %reduce-scatter.2.cloned.1.call-done = f32[512,128]{1,0:T(8,128)} async-done(((f32[4096,128]{1,0:T(8,128)}), f32[512,128]{1,0:T(8,128)}) %reduce-scatter.2.cloned.1.call-update) | async-done | bytes 262160 | tf_op jit(solution)/shard_map/reduce_scatter | solution.py:57
  348.2 0.0 copy-done
  348.2 1.0 sub.43
  349.2 5.7 %collective-permute-start = (f32[1,2,64,128]{3,2,1,0:T(8,128)S(1)}, f32[1,2,64,128]{3,2,1,0:T(8,128)S(1)}, u32[]{:S(2)}, u32[]{:S(2)}) collective-permute-start(f32[1,2,64,128]{3,2,1,0:T(8,128)S(1)} %get-tuple-element.12), channel_id=1, source_target_pairs={{16,0},{32,16},{48,32},{64,48},{80,64},{96,80},{112,96},{17,1},{33... | collective-permute-start | bytes 196616 | tf_op jit(solution)/shard_map/ppermute | solution.py:18
  354.9 1.9 collective-permute-start.1
  356.8 0.0 collective-permute-done
  356.9 1.3 collective-permute-done.1
  358.2 4.6 %collective-permute-start.2 = (f32[6,1,64,128]{3,2,1,0:T(8,128)S(1)}, f32[6,1,64,128]{3,2,1,0:T(8,128)S(1)}, u32[]{:S(2)}, u32[]{:S(2)}) collective-permute-start(f32[6,1,64,128]{3,2,1,0:T(8,128)S(1)} %get-tuple-element.8), channel_id=1, source_target_pairs={{1,0},{2,1},{3,2},{4,3},{5,4},{6,5},{7,6},{8,7},{9,8},{10,9},{11,1... | collective-permute-start | bytes 589832 | tf_op jit(solution)/shard_map/ppermute | solution.py:18
  362.8 1.9 collective-permute-start.3
  364.7 2.3 collective-permute-done.2
  367.0 5.9 %collective-permute-done.3 = f32[6,1,64,128]{3,2,1,0:T(8,128)S(1)} collective-permute-done((f32[6,1,64,128]{3,2,1,0:T(8,128)S(1)}, f32[6,1,64,128]{3,2,1,0:T(8,128)S(1)}, u32[]{:S(2)}, u32[]{:S(2)}) %collective-permute-start.3) | collective-permute-done | bytes 196640 | tf_op jit(solution)/shard_map/ppermute | solution.py:15
  372.9 0.1 select_maximum_fusion.4
  373.0 0.4 multiply_add_fusion.1
  373.5 3.1 collective-permute-start.4
  376.6 2.9 collective-permute-start.5
  379.5 0.0 collective-permute-done.4
  379.5 1.3 collective-permute-done.5
  380.9 1.9 collective-permute-start.6
  382.8 3.4 collective-permute-start.7
  386.2 3.1 collective-permute-done.6
  389.2 3.7 collective-permute-done.7
  392.9 0.1 select_maximum_fusion
  393.0 1.1 multiply_add_fusion
  (7 shorter events, 0.1 us)
Async XLA Ops:
  6.5 28.7 %all-gather.3.cloned.1.call-start = ((), (), s32[]{:S(2)}) async-start(), calls=%async_computation.1 | async-start | bytes 1179648 | tf_op jit(solution)/shard_map/all_gather | solution.py:40
  8.2 280.4 %all-gather.5.cloned.1.call-start = ((), (), s32[]{:S(2)}) async-start(), calls=%async_computation.2 | async-start | bytes 44564480 | tf_op jit(solution)/shard_map/all_gather | solution.py:50
  49.1 299.0 %reduce-scatter.2.cloned.1.call-start = ((), (), s32[]{:S(2)}) async-start(), calls=%async_computation.3 | async-start | bytes 2359296 | tf_op jit(solution)/shard_map/reduce_scatter | solution.py:57
  315.7 32.5 %copy-start = (f32[4,2,64,128]{3,2,1,0:T(8,128)S(1)}, f32[4,2,64,128]{3,2,1,0:T(8,128)}, u32[]{:S(2)}) copy-start(f32[4,2,64,128]{3,2,1,0:T(8,128)} %param.5) | copy-start | bytes 786436
  349.2 7.7 %collective-permute-start = (f32[1,2,64,128]{3,2,1,0:T(8,128)S(1)}, f32[1,2,64,128]{3,2,1,0:T(8,128)S(1)}, u32[]{:S(2)}, u32[]{:S(2)}) collective-permute-start(f32[1,2,64,128]{3,2,1,0:T(8,128)S(1)} %get-tuple-element.12), channel_id=1, source_target_pairs={{16,0},{32,16},{48,32},{64,48},{80,64},{96,80},{112,96},{17,1},{33... | collective-permute-start | bytes 196616 | tf_op jit(solution)/shard_map/ppermute | solution.py:18
  354.9 3.2 collective-permute-start.1
  358.2 8.8 %collective-permute-start.2 = (f32[6,1,64,128]{3,2,1,0:T(8,128)S(1)}, f32[6,1,64,128]{3,2,1,0:T(8,128)S(1)}, u32[]{:S(2)}, u32[]{:S(2)}) collective-permute-start(f32[6,1,64,128]{3,2,1,0:T(8,128)S(1)} %get-tuple-element.8), channel_id=1, source_target_pairs={{1,0},{2,1},{3,2},{4,3},{5,4},{6,5},{7,6},{8,7},{9,8},{10,9},{11,1... | collective-permute-start | bytes 589832 | tf_op jit(solution)/shard_map/ppermute | solution.py:18
  362.8 10.1 %collective-permute-start.3 = (f32[6,1,64,128]{3,2,1,0:T(8,128)S(1)}, f32[6,1,64,128]{3,2,1,0:T(8,128)S(1)}, u32[]{:S(2)}, u32[]{:S(2)}) collective-permute-start(f32[6,1,64,128]{3,2,1,0:T(8,128)S(1)} %get-tuple-element.7), channel_id=1, source_target_pairs={{0,1},{1,2},{2,3},{3,4},{4,5},{5,6},{6,7},{7,8},{8,9},{9,10},{10,1... | collective-permute-start | bytes 589832 | tf_op jit(solution)/shard_map/ppermute | solution.py:15
  373.5 6.0 %collective-permute-start.4 = (f32[1,2,64,128]{3,2,1,0:T(8,128)S(1)}, f32[1,2,64,128]{3,2,1,0:T(8,128)S(1)}, u32[]{:S(2)}, u32[]{:S(2)}) collective-permute-start(f32[1,2,64,128]{3,2,1,0:T(8,128)S(1)} %get-tuple-element.10), channel_id=1, source_target_pairs={{16,0},{32,16},{48,32},{64,48},{80,64},{96,80},{112,96},{17,1},{33... | collective-permute-start | bytes 196616 | tf_op jit(solution)/shard_map/ppermute | solution.py:18
  376.6 4.2 %collective-permute-start.5 = (f32[1,2,64,128]{3,2,1,0:T(8,128)S(1)}, f32[1,2,64,128]{3,2,1,0:T(8,128)S(1)}, u32[]{:S(2)}, u32[]{:S(2)}) collective-permute-start(f32[1,2,64,128]{3,2,1,0:T(8,128)S(1)} %get-tuple-element.9), channel_id=1, source_target_pairs={{0,16},{16,32},{32,48},{48,64},{64,80},{80,96},{96,112},{1,17},{17... | collective-permute-start | bytes 196616 | tf_op jit(solution)/shard_map/ppermute | solution.py:15
  380.9 8.4 %collective-permute-start.6 = (f32[6,1,64,128]{3,2,1,0:T(8,128)S(1)}, f32[6,1,64,128]{3,2,1,0:T(8,128)S(1)}, u32[]{:S(2)}, u32[]{:S(2)}) collective-permute-start(f32[6,1,64,128]{3,2,1,0:T(8,128)S(1)} %get-tuple-element.6), channel_id=1, source_target_pairs={{1,0},{2,1},{3,2},{4,3},{5,4},{6,5},{7,6},{8,7},{9,8},{10,9},{11,1... | collective-permute-start | bytes 589832 | tf_op jit(solution)/shard_map/ppermute | solution.py:18
  382.8 10.2 %collective-permute-start.7 = (f32[6,1,64,128]{3,2,1,0:T(8,128)S(1)}, f32[6,1,64,128]{3,2,1,0:T(8,128)S(1)}, u32[]{:S(2)}, u32[]{:S(2)}) collective-permute-start(f32[6,1,64,128]{3,2,1,0:T(8,128)S(1)} %get-tuple-element.5), channel_id=1, source_target_pairs={{0,1},{1,2},{2,3},{3,4},{4,5},{5,6},{6,7},{7,8},{8,9},{9,10},{10,1... | collective-permute-start | bytes 589832 | tf_op jit(solution)/shard_map/ppermute | solution.py:15
Sparse Core Ops, SparseCore 0:
  9.1 26.1 all-gather.2
  49.3 239.2 all-gather.4
  317.7 30.4 reduce-scatter.1
